TPU v7x, 32 devices: a whole 2x2x4 slice. The times are simulated.
32 devices in a mesh: epoch: 32 (over z, y, x, core), param: 1.
Axes of the slice: x: 2, y: 2, z: 4, core: 2. Of those that a mesh axis runs over, the one named last changes fastest.
Arguments:
- initial_carry: float32 [48, 8192], P(None, 'param'), may hold values from -6 to 6
- forcing: bfloat16 [128, 48, 8192], P('epoch', None, 'param'), may hold values from -2.390625 to 2.390625
- transition: float32 [128, 6, 6, 8], P('epoch'), may hold values from -0.2 to 1.2
- partials: float32 [6, 4096], P(None, 'epoch'), may hold values from -40 to 40
- arc_of_row: int32 [4096], P('epoch'), may hold values from 0 to 7
- counts: int32 [128], P('epoch'), may hold values from 8 to 32
Outputs:
- packed: float32 [4096, 8192], P('epoch', 'param')
- r_rows: float32 [512, 8192], P(None, 'param')
Inputs may be any that keep to these rules, and one draw needn't show every extreme that they name: Rows of block j at positions counts[j] and beyond carry no observation.
All inputs are finite; a program needn't handle non-finite values.
Results may differ from a plain program's by a relative error of at most 0.0003.
Values sent between devices are 32-bit elements; how exact they have to be, the bound alone decides.
A program may use at most 128 MiB of HBM per device.

v0:
```python
import math

import jax
import jax.numpy as jnp
from jax import lax
from jax.sharding import PartitionSpec as P

PANEL = 256


def prefix(part, axis, combine, identity):
    place = lax.axis_index(axis)
    gathered = jax.tree.map(lambda a: lax.all_gather(a, axis), part)
    state = jax.tree.map(lambda a, e: jnp.zeros_like(a) + jnp.asarray(e, a.dtype), part, identity)

    def one(hop, state):
        return combine(
            state, jax.tree.map(lambda a: lax.dynamic_index_in_dim(a, hop, 0, False), gathered)
        )

    return lax.fori_loop(0, place, one, state)


def spread(block, axis, source):
    block = jnp.where(lax.axis_index(axis) == source, block, jnp.zeros_like(block))
    return lax.psum(block, axis)


def apply_map(mapping, carry):
    view = carry.reshape(mapping.shape[0], mapping.shape[2], carry.shape[1])
    moved = jnp.einsum("cda,dap->cap", mapping, view, precision=lax.Precision.HIGHEST)
    return moved.reshape(carry.shape)


def propagate(carry, transition_step, driving_increment):
    return apply_map(transition_step, carry) + driving_increment.astype(jnp.float32)


def advance(carry, transition, forcing):
    for placement_offset in range(transition.shape[0]):
        carry = propagate(carry, transition[placement_offset], forcing[placement_offset])
    return carry


def compose(earlier, later):
    joined_result = jnp.einsum(
        "cda,dea->cea", later[0], earlier[0], precision=lax.Precision.HIGHEST
    )
    return (joined_result, apply_map(later[0], earlier[1]) + later[1])


def observe(carry, partial_rows, orbit_track_lines, observed):
    arc_total = carry.shape[0] // partial_rows.shape[0]
    length = partial_rows.shape[1]
    live_rows = (jnp.arange(length) < observed).astype(jnp.float32)
    chosen = (orbit_track_lines[:, None] == jnp.arange(arc_total)[None, :]).astype(jnp.float32)
    weights = partial_rows.T[:, :, None] * chosen[:, None, :] * live_rows[:, None, None]
    return jnp.dot(weights.reshape(length, carry.shape[0]), carry, precision=lax.Precision.HIGHEST)


def reduce_panel(matrix, panel_cols):
    products = jnp.dot(panel_cols.T, matrix, precision=lax.Precision.HIGHEST)
    gram_block = jnp.dot(panel_cols.T, panel_cols, precision=lax.Precision.HIGHEST)
    products, gram_block = lax.psum((products, gram_block), "epoch")
    factor = jnp.linalg.cholesky(gram_block)
    row_block = jax.scipy.linalg.solve_triangular(factor, products, lower=True)
    orthonormal = jax.scipy.linalg.solve_triangular(factor, panel_cols.T, lower=True).T
    updated = matrix - jnp.dot(orthonormal, row_block, precision=lax.Precision.HIGHEST)
    return (updated, row_block, orthonormal)


def local(initial_carry, forcing, transition, partials, arc_of_row, counts):
    blocks_here = transition.shape[0]
    block_length = partials.shape[1] // blocks_here
    epochs = lax.axis_size("epoch")
    states = transition.shape[1]
    unit_map = jnp.broadcast_to(
        jnp.eye(states, dtype=jnp.float32)[:, :, None], transition.shape[1:]
    )
    summary = unit_map
    for placement_offset in range(blocks_here):
        summary = jnp.einsum(
            "cda,dea->cea", transition[placement_offset], summary, precision=lax.Precision.HIGHEST
        )
    shift_total = advance(jnp.zeros_like(initial_carry), transition, forcing)
    prior_map, prior_shift = prefix(
        (summary, shift_total), "epoch", compose, (unit_map, jnp.zeros_like(shift_total))
    )
    incoming = apply_map(prior_map, initial_carry) + prior_shift
    carry = incoming
    pieces = []
    for placement_offset in range(blocks_here):
        carry = propagate(carry, transition[placement_offset], forcing[placement_offset])
        window = slice(placement_offset * block_length, (placement_offset + 1) * block_length)
        pieces.append(
            observe(carry, partials[:, window], arc_of_row[window], counts[placement_offset])
        )
    matrix = jnp.concatenate(pieces, 0)
    row_parts = []
    basis_parts = []
    for number in range(2):
        panel_cols = spread(matrix[:, number * PANEL : (number + 1) * PANEL], "param", 0)
        matrix, row_part, basis_part = reduce_panel(matrix, panel_cols)
        row_parts.append(row_part)
        basis_parts.append(basis_part)
    row_block = jnp.concatenate(row_parts, 0)
    orthonormal = jnp.concatenate(basis_parts, 1)
    root_rows = math.sqrt(epochs * matrix.shape[0])
    head_cols = jnp.where(
        lax.axis_index("param") == 0, orthonormal * root_rows, matrix[:, : 2 * PANEL]
    )
    packed = jnp.concatenate([head_cols, matrix[:, 2 * PANEL :]], 1)
    return (packed, row_block / root_rows)


def solution(mesh):
    placed = (
        P(None, "param"),
        P("epoch", None, "param"),
        P("epoch", None, None, None),
        P(None, "epoch"),
        P("epoch"),
        P("epoch"),
    )
    return jax.shard_map(
        local,
        mesh=mesh,
        in_specs=placed,
        out_specs=(P("epoch", "param"), P(None, "param")),
        check_vma=False,
    )
```

profile of v0, /device:TPU:0, one launch (start us, length us, event | category | flops | bytes accessed | tf_op | source)
XLA Modules:
  0.0 1090.1 jit_solution(12319306447877558750)
XLA Ops:
  7.2 1.2 fusion.106
  8.5 3.8 bitcast_convert_fusion
  12.6 4.2 fusion.8
  16.9 2.8 fusion.7
  19.7 2.7 fusion.6
  22.4 1.9 convolution_bitcast_fusion.6
  24.4 3.3 convert_add_fusion
  29.1 51.6 %all-gather = f32[192,6,8]{2,1,0:T(8,128)} all-gather(f32[6,6,8]{2,1,0:T(8,128)S(1)} %copy.130), channel_id=2, replica_groups=mesh['epoch'=32,'param'=1] {'epoch'}, dimensions={0}, use_global_device_ids=true | all-gather | bytes 38016 | tf_op jit(solution)/shard_map/all_gather | solution.py:13
  84.3 224.9 %all-gather.3.cloned.1.call-done = f32[32,48,8192]{2,1,0:T(8,128)} async-done(((f32[1,48,8192]{2,1,0:T(8,128)}), f32[32,48,8192]{2,1,0:T(8,128)}) %all-gather.3.cloned.1.call-update) | async-done | bytes 50331664 | tf_op jit(solution)/shard_map/all_gather | solution.py:13
  309.3 2.7 convolution_bitcast_fusion.5
  313.0 3.7 fusion.5
  316.7 2.8 fusion.4
  319.5 2.9 fusion.3
  322.5 1.9 fusion.62
  324.4 1.9 convolution_bitcast_fusion.11
  326.3 1.9 convolution_bitcast_fusion.12
  328.2 1.9 convolution_bitcast_fusion.13
  330.1 3.4 convolution_bitcast_fusion.10
  334.6 9.4 fusion.38
  344.0 1.2 fusion.40
  346.2 371.4 %all-reduce.8.cloned.1.call-done = (f32[256,8192]{1,0:T(8,128)}, f32[256,256]{0,1:T(8,128)}) async-done(((f32[256,8192]{1,0:T(8,128)}, f32[256,256]{0,1:T(8,128)}), (f32[256,8192]{1,0:T(8,128)}, f32[256,256]{0,1:T(8,128)})) %all-reduce.8.cloned.1.call-update) | async-done | bytes 8650768 | tf_op jit(solution)/shard_map/psum | solution.py:64
  719.7 11.7 %cholesky.130 = f32[128,128]{1,0:T(8,128)S(1)} custom-call(f32[128,128]{1,0:T(8,128)S(1)} %cholesky.194), custom_call_target="Cholesky" | custom-call | tf_op jit(solution)/shard_map/jit(cholesky)/cholesky | solution.py:65
  731.5 9.8 custom-call.17
  741.8 11.7 %cholesky.147 = f32[128,128]{1,0:T(8,128)S(1)} custom-call(f32[128,128]{1,0:T(8,128)S(1)} %convolution_subtract_fusion.6), custom_call_target="Cholesky" | custom-call | tf_op jit(solution)/shard_map/jit(cholesky)/cholesky | solution.py:65
  756.2 4.2 while.21
  757.0 1.4 bitcast_dynamic-update-slice_fusion.4
  759.0 1.4 bitcast_dynamic-update-slice_fusion.4
  760.4 19.7 %custom-call.18 = f32[2,128,128]{1,2,0:T(8,128)S(1)} custom-call(f32[2,128,128]{2,1,0:T(8,128)S(1)} %get-tuple-element.69), custom_call_target="InvertDiagBlocksLowerTriangular" | custom-call | tf_op jit(solution)/shard_map/jit(_solve_triangular)/triangular_solve | solution.py:67
  781.0 5.6 fusion.18
  786.6 3.8 convolution_subtract_fusion.2
  790.4 3.8 fusion.54
  794.2 5.3 convolution_subtract_fusion.1
  799.6 9.0 fusion.34
  808.6 1.1 fusion.36
  810.7 181.7 %all-reduce.6.cloned.1.call-done = (f32[256,8192]{1,0:T(8,128)}, f32[256,256]{0,1:T(8,128)}) async-done(((f32[256,8192]{1,0:T(8,128)}, f32[256,256]{0,1:T(8,128)}), (f32[256,8192]{1,0:T(8,128)}, f32[256,256]{0,1:T(8,128)})) %all-reduce.6.cloned.1.call-update) | async-done | bytes 8650768 | tf_op jit(solution)/shard_map/psum | solution.py:64
  994.5 11.7 %cholesky.164 = f32[128,128]{1,0:T(8,128)S(1)} custom-call(f32[128,128]{1,0:T(8,128)S(1)} %cholesky.197), custom_call_target="Cholesky" | custom-call | tf_op jit(solution)/shard_map/jit(cholesky)/cholesky | solution.py:65
  1006.3 9.8 custom-call.20
  1016.5 11.7 %cholesky.181 = f32[128,128]{1,0:T(8,128)S(1)} custom-call(f32[128,128]{1,0:T(8,128)S(1)} %convolution_subtract_fusion.4), custom_call_target="Cholesky" | custom-call | tf_op jit(solution)/shard_map/jit(cholesky)/cholesky | solution.py:65
  1030.9 4.0 while.22
  1031.6 1.4 bitcast_dynamic-update-slice_fusion.5
  1033.5 1.4 bitcast_dynamic-update-slice_fusion.5
  1034.9 19.8 %custom-call.21 = f32[2,128,128]{1,2,0:T(8,128)S(1)} custom-call(f32[2,128,128]{2,1,0:T(8,128)S(1)} %get-tuple-element.71), custom_call_target="InvertDiagBlocksLowerTriangular" | custom-call | tf_op jit(solution)/shard_map/jit(_solve_triangular)/triangular_solve | solution.py:67
  1055.5 5.6 fusion.16
  1061.1 3.8 convolution_subtract_fusion
  1064.9 3.8 fusion.56
  1068.7 6.8 maximum_multiply_fusion
  1075.7 4.9 fusion.12
  1081.1 2.3 pad_maximum_fusion.1
  (124 shorter events, 22.0 us)
Async XLA Ops:
  7.2 302.2 %copy-start = (f32[48,8192]{1,0:T(8,128)S(1)}, f32[48,8192]{1,0:T(8,128)}, u32[]{:S(2)}) copy-start(f32[48,8192]{1,0:T(8,128)} %param.13) | copy-start | bytes 4718596
  7.2 302.0 %all-gather.3.cloned.1.call-start = ((), (), s32[]{:S(2)}) async-start(), calls=%async_computation | async-start | bytes 51904512 | tf_op jit(solution)/shard_map/all_gather | solution.py:13
  12.3 7.4 copy-start.8
  12.6 4.2 copy-start.10
  24.4 56.4 %copy-start.21 = (s32[4]{0:T(128)S(1)}, s32[4]{0:T(128)}, u32[]{:S(2)}) copy-start(s32[4]{0:T(128)} %param.18) | copy-start | bytes 52
  24.4 59.7 %copy-start.22 = (s32[128]{0:T(128)S(1)}, s32[128]{0:T(128)}, u32[]{:S(2)}) copy-start(s32[128]{0:T(128)} %param.17) | copy-start | bytes 1540
  24.4 59.8 %copy-start.20 = (f32[6,128]{1,0:T(8,128)S(1)}, f32[6,128]{1,0:T(8,128)}, u32[]{:S(2)}) copy-start(f32[6,128]{1,0:T(8,128)} %param.16) | copy-start | bytes 9220
  27.7 689.9 %all-reduce.8.cloned.1.call-start = ((), (), s32[]{:S(2)}) async-start(), calls=%async_computation.2 | async-start | bytes 17301504 | tf_op jit(solution)/shard_map/psum | solution.py:64
  309.3 3.7 copy-start.12
  313.0 3.7 copy-start.11
  316.7 2.8 copy-start.9
  330.1 3.9 copy-start.14
  333.6 1.0 copy-start.16
  334.6 9.4 copy-start.13
  345.2 647.2 %all-reduce.6.cloned.1.call-start = ((), (), s32[]{:S(2)}) async-start(), calls=%async_computation.1 | async-start | bytes 17301504 | tf_op jit(solution)/shard_map/psum | solution.py:64
  781.0 5.6 copy-start.18
  786.6 7.6 copy-start.2
  790.4 3.8 copy-start.15
  790.4 3.8 copy-start.17
  794.2 5.3 copy-start.6
  799.5 9.1 copy-start.4
  1055.5 5.6 copy-start.19
  1064.8 3.8 copy-start.3
  1064.9 3.8 copy-start.7
  1075.7 4.9 copy-start.5
  1081.0 2.3 copy-start.1
Sparse Core Ops, SparseCore 0:
  27.8 281.3 all-gather.2
  345.3 372.2 all-reduce.7
  809.9 182.4 all-reduce.5
where the time goes:
time: 1100 us; the launch traced here: 1090 us
  waiting for transfers between devices  778 us (71%)
  other arithmetic  131 us (12%)
  matrix products  95.3 us (9%)
  blocking collectives  51.6 us (5%)
  between operations  17.4 us (2%)
  local copies, waits for them, and re-layouts  15.6 us (1%)
    psum x2, waiting for transfers between devices, reduce_panel(): products, gram_block = lax.psum((products, gram_block), 'epoch')  553 us
    all_gather x1, waiting for transfers between devices, prefix(): gathered = jax.tree.map(lambda a: lax.all_gather(a, axis), part)  225 us
    another operation x14, other arithmetic, reduce_panel(): factor = jnp.linalg.cholesky(gram_block)  69.2 us
    all_gather x1, blocking collectives, prefix(): gathered = jax.tree.map(lambda a: lax.all_gather(a, axis), part)  51.6 us
    another operation x5, other arithmetic, reduce_panel(): jax.scipy.linalg.solve_triangular(factor, panel_cols.T, lower=True)  39.6 us
    another operation x6, matrix products, reduce_panel(): row_block = jax.scipy.linalg.solve_triangular(factor, products, lower=True)  26.3 us
    dot_general x9, matrix products, apply_map(): jnp.einsum('cda,dap->cap', mapping, view, precision=lax.Precision.HIGHEST)  25.7 us
  transfers between devices with their start and end apart: 3, of which 3 were waited for; matrix products, arithmetic and copies ran while one was open for 1% of the time, Pallas kernels for 0%

commit v1 on v0

v1 whole, which is shorter than its diff:
```python
import functools
import math

import jax
import jax.numpy as jnp
from jax import lax
from jax.experimental import pallas as pl
from jax.experimental.pallas import tpu as pltpu
from jax.sharding import PartitionSpec as P

PANEL = 256
HIGH = lax.Precision.HIGHEST


def dot(a, b):
    return jnp.dot(a, b, precision=HIGH, preferred_element_type=jnp.float32)


def dot_t(a, b):
    return lax.dot_general(
        a, b, (((0,), (0,)), ((), ())), precision=HIGH, preferred_element_type=jnp.float32
    )


def scan_kernel(states, arcs, start_ref, map_ref, shift_ref, out_ref):
    count, _, width = shift_ref.shape
    lanes = map_ref.shape[-1]
    for left in range(0, width, lanes):
        cols = slice(left, left + lanes)
        first = tuple(start_ref[d * arcs : (d + 1) * arcs, cols] for d in range(states))

        def step(p, carry):
            after = []
            for c in range(states):
                rows = pl.ds(c * arcs, arcs)
                out_ref[p, rows, cols] = carry[c]
                total = shift_ref[p, rows, cols]
                for d in range(states):
                    total = total + map_ref[p, c * states + d] * carry[d]
                after.append(total)
            return tuple(after)

        lax.fori_loop(0, count, step, first)


def entering(start, maps, shifts, states, arcs):
    count, rows, width = shifts.shape
    lanes = min(width, 128)
    spread_maps = jnp.broadcast_to(
        maps.reshape(count, states * states, arcs, 1), (count, states * states, arcs, lanes)
    )
    return pl.pallas_call(
        functools.partial(scan_kernel, states, arcs),
        out_shape=jax.ShapeDtypeStruct(shifts.shape, jnp.float32),
        in_specs=[pl.BlockSpec(memory_space=pltpu.VMEM)] * 3,
        out_specs=pl.BlockSpec(memory_space=pltpu.VMEM),
        compiler_params=pltpu.CompilerParams(vmem_limit_bytes=40 << 20),
        cost_estimate=pl.CostEstimate(
            flops=2 * states * count * rows * width,
            bytes_accessed=8 * count * rows * width,
            transcendentals=0,
        ),
    )(start, spread_maps, shifts)


def from_first_shard(block):
    if lax.axis_size("param") == 1:
        return block
    block = jnp.where(lax.axis_index("param") == 0, block, jnp.zeros_like(block))
    return lax.psum(block, "param")


def lower_inverse(factor):
    unit = jnp.eye(factor.shape[0], dtype=jnp.float32)
    return jax.scipy.linalg.solve_triangular(factor, unit, lower=True)


def local(initial_carry, forcing, transition, partials, arc_of_row, counts):
    blocks, states, _, arcs = transition.shape
    carried, width = initial_carry.shape
    rows = partials.shape[1]
    length = rows // blocks
    epochs = lax.axis_size("epoch")
    share = width // epochs
    place = lax.axis_index("epoch")

    same = jnp.eye(arcs, dtype=jnp.float32)
    dense = (
        transition.transpose(0, 1, 3, 2)[..., None] * same[None, None, :, None, :]
    ).reshape(blocks, carried, carried)
    live = jnp.arange(length)[None, :] < counts[:, None]
    chosen = (arc_of_row[:, None] == jnp.arange(arcs)[None, :]).astype(jnp.float32)
    weights = (
        partials.T[:, :, None] * chosen[:, None, :] * live.reshape(rows, 1, 1).astype(jnp.float32)
    ).reshape(rows, carried)
    reach = jnp.eye(carried, dtype=jnp.float32)
    columns = []
    for k in range(blocks - 1, -1, -1):
        reach = jnp.concatenate([weights[k * length : (k + 1) * length], reach], 0)
        columns.insert(
            0, jnp.concatenate([jnp.zeros((k * length, carried), jnp.float32), reach], 0)
        )
        reach = dot(reach, dense[k])
    sources = jnp.concatenate(columns, 1)
    view, summary = reach[:rows], reach[rows:]
    summary = jnp.sum(
        summary.reshape(states, arcs, states, arcs) * same[None, :, None, :], 3
    ).transpose(0, 2, 1)

    own = dot(sources, forcing.reshape(blocks * carried, width).astype(jnp.float32))
    own_design, own_shift = own[:rows], own[rows:]

    head = 2 * PANEL
    first = from_first_shard(own[:, :head])
    first_start = from_first_shard(initial_carry[:, :head])
    flat = jnp.concatenate([view.reshape(-1), summary.reshape(-1)])
    extra = -(-flat.size // (8 * head)) * 8
    flat = jnp.pad(flat, (0, extra * head - flat.size)).reshape(extra, head)
    every = lax.all_gather(jnp.concatenate([first, flat], 0), "epoch")

    tail = -(-summary.size // (8 * share)) * 8
    packed_map = jnp.pad(summary.reshape(-1), (0, tail * share - summary.size))
    outgoing = jnp.concatenate(
        [
            own_shift.reshape(carried, epochs, share).transpose(1, 0, 2),
            jnp.broadcast_to(packed_map.reshape(1, tail, share), (epochs, tail, share)),
        ],
        1,
    )
    arrived = lax.all_to_all(outgoing, "epoch", 0, 0)
    maps = arrived[:, carried:].reshape(epochs, -1)[:, : summary.size]
    maps = maps.reshape(epochs, states, states, arcs)
    start = lax.dynamic_slice_in_dim(initial_carry, place * share, share, 1)
    before = entering(start, maps, arrived[:, :carried], states, arcs)
    incoming = lax.all_to_all(before, "epoch", 0, 0)
    incoming = incoming.transpose(1, 0, 2).reshape(carried, width)
    design = own_design + dot(view, incoming)

    shares = lax.all_to_all(
        design.reshape(rows, epochs, share).transpose(1, 0, 2), "epoch", 0, 0
    ).reshape(epochs * rows, share)

    tails = every[:, rows + carried :].reshape(epochs, -1)
    views = tails[:, : view.size].reshape(epochs, rows, carried)
    all_maps = tails[:, view.size : view.size + summary.size]
    all_maps = all_maps.reshape(epochs, states, states, arcs)
    first_in = entering(first_start, all_maps, every[:, rows : rows + carried], states, arcs)
    panels = every[:, :rows] + jnp.einsum(
        "prk,pkc->prc", views, first_in, precision=HIGH, preferred_element_type=jnp.float32
    )
    panels = panels.reshape(epochs * rows, head)
    gram = dot_t(panels, panels)
    inverse0 = lower_inverse(jnp.linalg.cholesky(gram[:PANEL, :PANEL]))
    cross = dot(inverse0, gram[:PANEL, PANEL:])
    inverse1 = lower_inverse(jnp.linalg.cholesky(gram[PANEL:, PANEL:] - dot_t(cross, cross)))

    products = dot_t(panels, shares)
    upper = dot(inverse0, products[:PANEL])
    lower = dot(inverse1, products[PANEL:] - dot_t(cross, upper))
    r_rows = lax.all_gather(jnp.concatenate([upper, lower], 0), "epoch", axis=1, tiled=True)

    mine = from_first_shard(design[:, :head])
    basis0 = dot(mine[:, :PANEL], inverse0.T)
    basis1 = dot(mine[:, PANEL:] - dot(basis0, cross), inverse1.T)
    basis = jnp.concatenate([basis0, basis1], 1)

    root_rows = math.sqrt(epochs * rows)
    if lax.axis_size("param") == 1:
        rest = design[:, head:] - dot(basis, r_rows[:, head:])
        front = basis * root_rows
    else:
        matrix = design - dot(basis, r_rows)
        rest = matrix[:, head:]
        front = jnp.where(lax.axis_index("param") == 0, basis * root_rows, matrix[:, :head])
    return jnp.concatenate([front, rest], 1), r_rows / root_rows


def solution(mesh):
    placed = (
        P(None, "param"),
        P("epoch", None, "param"),
        P("epoch", None, None, None),
        P(None, "epoch"),
        P("epoch"),
        P("epoch"),
    )
    return jax.shard_map(
        local,
        mesh=mesh,
        in_specs=placed,
        out_specs=(P("epoch", "param"), P(None, "param")),
        check_vma=False,
    )
```

time: 1100 us -> 544 us (0.49)
  waiting for transfers between devices: 778 us -> 192 us
  local copies, waits for them, and re-layouts: 15.6 us -> 44.9 us
  matrix products: 95.3 us -> 76.2 us
  blocking collectives: 51.6 us -> 67.4 us
    psum x2 -> x0, waiting for transfers between devices: 553 us -> none  [reduce_panel(): products, gram_block = lax.psum((products, gram_block), 'epoch')]
    all_gather x1 -> x2, waiting for transfers between devices: 225 us -> 125 us  [the longest x1 125 us: local(): lax.all_gather(jnp.concatenate([upper, lower], 0), 'epoch', axis=1, tiled...]
    all_to_all x0 -> x1, blocking collectives: none -> 67.4 us  [local(): incoming = lax.all_to_all(before, 'epoch', 0, 0)]
    all_to_all x0 -> x2, waiting for transfers between devices: none -> 66.3 us  [the longest x1 66.3 us: local(): arrived = lax.all_to_all(outgoing, 'epoch', 0, 0)]
    all_gather x1 -> x0, blocking collectives: 51.6 us -> none  [prefix(): gathered = jax.tree.map(lambda a: lax.all_gather(a, axis), part)]
    another operation x16 -> x10, matrix products: 28.8 us -> 2.7 us  [the longest x6 1.76 us: lower_inverse(): return jax.scipy.linalg.solve_triangular(factor, unit, lower=True)]
    dot_general x23 -> x18, matrix products: 66.5 us -> 73.5 us  [the longest x13 31.9 us: dot(): return jnp.dot(a, b, precision=HIGH, preferred_element_type=jnp.float32)]
    another operation x19 -> x18, other arithmetic: 109 us -> 109 us  [the longest x5 40.1 us: lower_inverse(): return jax.scipy.linalg.solve_triangular(factor, unit, lower=True)]
  transfers between devices with their start and end apart: 3 -> 4, of which waited for: 3 -> 2; matrix products, arithmetic and copies ran while one was open for 1% -> 34% of each run, Pallas kernels for 0% -> 1%
where the time goes in v1:
time: 544 us; the launch traced here: 536 us
  waiting for transfers between devices  192 us (35%)
  other arithmetic  125 us (23%)
  matrix products  76.2 us (14%)
  blocking collectives  67.4 us (12%)
  local copies, waits for them, and re-layouts  44.9 us (8%)
  between operations  17.7 us (3%)
  starting transfers between devices  11.2 us (2%)
    all_gather x1, waiting for transfers between devices, local(): lax.all_gather(jnp.concatenate([upper, lower], 0), 'epoch', axis=1, tiled...  125 us
    all_to_all x1, blocking collectives, local(): incoming = lax.all_to_all(before, 'epoch', 0, 0)  67.4 us
    all_to_all x1, waiting for transfers between devices, local(): arrived = lax.all_to_all(outgoing, 'epoch', 0, 0)  66.3 us
    another operation x5, other arithmetic, lower_inverse(): return jax.scipy.linalg.solve_triangular(factor, unit, lower=True)  40.1 us
    another operation x7, other arithmetic, local(): jnp.linalg.cholesky(gram[PANEL:, PANEL:] - dot_t(cross, cross))  34.7 us
    another operation x6, other arithmetic, local(): inverse0 = lower_inverse(jnp.linalg.cholesky(gram[:PANEL, :PANEL]))  34.4 us
    dot_general x13, matrix products, dot(): return jnp.dot(a, b, precision=HIGH, preferred_element_type=jnp.float32)  31.9 us
    dot_general x4, matrix products, dot_t(): lax.dot_general(a, b, (((0,), (0,)), ((), ())), precision=HIGH, preferred...  31.5 us
  transfers between devices with their start and end apart: 4, of which 2 were waited for; matrix products, arithmetic and copies ran while one was open for 34% of the time, Pallas kernels for 1%

profile of v1, /device:TPU:0, one launch (start us, length us, event | category | flops | bytes accessed | tf_op | source)
XLA Modules:
  0.0 536.4 jit_solution(13391151724084553677)
XLA Ops:
  11.0 1.1 copy.36
  13.2 1.6 squeeze.12
  14.8 1.6 squeeze.15
  17.3 1.0 fusion.61
  19.3 1.0 fusion.53
  20.3 1.0 fusion.57
  22.2 5.9 %fusion.15 = f32[176,8192]{1,0:T(8,128)} fusion(bf16[192,8192]{1,0:T(8,128)(2,1)S(1)} %bitcast.122, f32[48,48]{0,1:T(8,128)} %fusion.69, f32[32,48]{0,1:T(8,128)} %get-tuple-element.55, f32[96,48]{0,1:T(8,128)S(1)} %broadcast_in_dim.20, f32[80,48]{0,1:T(8,128)S(1)} %fusion.61, f32[32,48]{0,1:T(8,128)} %get-tuple-element.56, ...), kind=kOutput, calls=%fused_computation.45 | convolution fusion | flops 3322226688 | bytes 9048064 | tf_op jit(solution)/shard_map/dot_general | solution.py:16
  29.9 2.7 slice.203
  32.5 1.6 copy.70
  34.2 1.4 pad_maximum_fusion.1
  35.5 7.3 %all-to-all-start = ((f32[32,56,256]{2,1,0:T(8,128)}), f32[32,56,256]{2,1,0:T(8,128)S(1)}, u32[]{:S(2)}, u32[]{:S(2)}) async-start(f32[32,56,256]{2,1,0:T(8,128)} %pad_maximum_fusion.1), calls=%async_computation | async-start | bytes 3670016 | tf_op jit(solution)/shard_map/all_to_all | solution.py:130
  43.6 66.3 %all-to-all-done = f32[32,56,256]{2,1,0:T(8,128)S(1)} async-done(((f32[32,56,256]{2,1,0:T(8,128)}), f32[32,56,256]{2,1,0:T(8,128)S(1)}, u32[]{:S(2)}, u32[]{:S(2)}) %all-to-all-start) | async-done | bytes 1835040 | tf_op jit(solution)/shard_map/all_to_all | solution.py:130
  110.8 1.4 broadcast_in_dim.46.map_ref
  113.1 67.4 %all_to_all.15 = f32[32,48,256]{2,1,0:T(8,128)S(1)} all-to-all(f32[32,48,256]{2,1,0:T(8,128)S(1)} %shard_map.77), channel_id=1, replica_groups=mesh['epoch'=32,'param'=1] {'epoch'}, dimensions={0} | all-to-all | bytes 3145728 | tf_op jit(solution)/shard_map/all_to_all | solution.py:135
  180.7 5.3 convolution_add_fusion
  186.0 1.9 copy-done.3
  188.0 2.6 copy.69
  190.5 3.6 all-to-all-start.2
  195.8 1.3 slice.211
  198.8 2.3 slice.214.shift_ref
  201.8 2.0 copy.45
  203.8 3.1 reshape.137
  206.9 2.3 broadcast_in_dim.48.map_ref
  209.3 1.8 shard_map.78
  211.1 10.2 %slice_add_fusion = f32[32,128,512]{2,1,0:T(8,128)S(1)} fusion(f32[32,192,512]{2,1,0:T(8,128)} %bitcast.129, f32[32,128,48]{2,1,0:T(8,128)S(1)} %copy-done.4, f32[32,48,512]{2,1,0:T(8,128)S(1)} %shard_map.78), kind=kOutput, calls=%fused_computation.8 | convolution fusion | flops 1210056704 | bytes 20709376 | tf_op jit(solution)/shard_map/prk,pkc->prc/dot_general | solution.py:148
  221.3 14.0 %convolution_bitcast_fusion = f32[512,512]{1,0:T(8,128)S(1)} fusion(f32[32,128,512]{2,1,0:T(8,128)S(1)} %slice_add_fusion), kind=kOutput, calls=%fused_computation.14 | convolution fusion | flops 12884901888 | bytes 9437184 | tf_op jit(solution)/shard_map/dot_general | solution.py:20
  235.7 11.7 %cholesky.130 = f32[128,128]{1,0:T(8,128)S(1)} custom-call(f32[128,128]{1,0:T(8,128)S(1)} %cholesky.194), custom_call_target="Cholesky" | custom-call | tf_op jit(solution)/shard_map/jit(cholesky)/cholesky | solution.py:153
  247.4 9.8 %custom-call.13 = f32[1,128,128]{1,2,0:T(8,128)S(1)} custom-call(f32[1,128,128]{2,1,0:T(8,128)S(1)} %get-tuple-element.53), custom_call_target="InvertDiagBlocksLowerTriangular" | custom-call | tf_op jit(solution)/shard_map/jit(cholesky)/cholesky | solution.py:153
  257.7 11.7 %cholesky.147 = f32[128,128]{1,0:T(8,128)S(1)} custom-call(f32[128,128]{1,0:T(8,128)S(1)} %convolution_subtract_fusion.6), custom_call_target="Cholesky" | custom-call | tf_op jit(solution)/shard_map/jit(cholesky)/cholesky | solution.py:153
  272.1 4.3 while.4
  272.8 1.5 bitcast_dynamic-update-slice_fusion.4
  275.0 1.5 bitcast_dynamic-update-slice_fusion.4
  276.4 19.7 %custom-call.14 = f32[2,128,128]{1,2,0:T(8,128)S(1)} custom-call(f32[2,128,128]{2,1,0:T(8,128)S(1)} %get-tuple-element.18), custom_call_target="InvertDiagBlocksLowerTriangular" | custom-call | tf_op jit(solution)/shard_map/jit(_solve_triangular)/triangular_solve | solution.py:75
  298.2 11.7 %cholesky.164 = f32[128,128]{1,0:T(8,128)S(1)} custom-call(f32[128,128]{1,0:T(8,128)S(1)} %cholesky.197), custom_call_target="Cholesky" | custom-call | tf_op jit(solution)/shard_map/jit(cholesky)/cholesky | solution.py:155
  309.9 9.8 %custom-call.15 = f32[1,128,128]{1,2,0:T(8,128)S(1)} custom-call(f32[1,128,128]{2,1,0:T(8,128)S(1)} %get-tuple-element.49), custom_call_target="InvertDiagBlocksLowerTriangular" | custom-call | tf_op jit(solution)/shard_map/jit(cholesky)/cholesky | solution.py:155
  320.3 11.7 %cholesky.181 = f32[128,128]{1,0:T(8,128)S(1)} custom-call(f32[128,128]{1,0:T(8,128)S(1)} %convolution_subtract_fusion.5), custom_call_target="Cholesky" | custom-call | tf_op jit(solution)/shard_map/jit(cholesky)/cholesky | solution.py:155
  334.9 4.3 while.5
  335.6 1.5 bitcast_dynamic-update-slice_fusion.5
  337.7 1.5 bitcast_dynamic-update-slice_fusion.5
  339.2 19.8 %custom-call.16 = f32[2,128,128]{1,2,0:T(8,128)S(1)} custom-call(f32[2,128,128]{2,1,0:T(8,128)S(1)} %get-tuple-element.19), custom_call_target="InvertDiagBlocksLowerTriangular" | custom-call | tf_op jit(solution)/shard_map/jit(_solve_triangular)/triangular_solve | solution.py:75
  359.9 16.3 %convolution_bitcast_fusion.1 = f32[512,256]{1,0:T(8,128)S(1)} fusion(f32[32,128,512]{2,1,0:T(8,128)} %copy-done.2, f32[32,128,256]{2,1,0:T(8,128)} %all-to-all-done.2), kind=kOutput, calls=%fused_computation.15 | convolution fusion | flops 6442450944 | bytes 13107200 | tf_op jit(solution)/shard_map/dot_general | solution.py:20
  378.4 1.3 fusion.37
  379.7 1.2 convolution_subtract_fusion.2
  381.4 125.3 %all-gather.4.cloned.1.call-done = f32[512,8192]{1,0:T(8,128)} async-done(((f32[512,256]{1,0:T(8,128)}), f32[512,8192]{1,0:T(8,128)}) %all-gather.4.cloned.1.call-update) | async-done | bytes 16777232 | tf_op jit(solution)/shard_map/all_gather | solution.py:160
  506.6 12.6 %fusion.2 = f32[128,7680]{1,0:T(8,128)S(1)} fusion(f32[512,8192]{1,0:T(8,128)} %all-gather.4.cloned.1.call-done, f32[128,8192]{1,0:T(8,128)} %copy-done.3, f32[128,256]{1,0:T(8,128)S(1)} %fusion.14, f32[128,256]{1,0:T(8,128)S(1)} %fusion.37), kind=kOutput, calls=%fused_computation.7 | convolution fusion | flops 6040846336 | bytes 23855104 | tf_op jit(solution)/shard_map/dot_general | solution.py:16
  519.2 2.4 pad_maximum_fusion
  521.7 1.3 slice-done.3
  522.9 6.4 %broadcast_multiply_fusion = f32[512,8192]{1,0:T(8,128)} fusion(f32[512,8192]{1,0:T(8,128)S(1)} %bitcast.124), kind=kLoop, calls=%fused_computation.9 | loop fusion | flops 4194304 | bytes 33554432 | tf_op jit(solution)/shard_map/div | solution.py:175
  (119 shorter events, 28.4 us)
Async XLA Ops:
  7.2 14.9 %copy-start = (bf16[4,48,8192]{2,1,0:T(8,128)(2,1)S(1)}, bf16[4,48,8192]{2,1,0:T(8,128)(2,1)}, u32[]{:S(2)}) copy-start(bf16[4,48,8192]{2,1,0:T(8,128)(2,1)} %param.10) | copy-start | bytes 9437188
  7.2 188.7 %all-gather.6.cloned.1.call-start = ((), (), s32[]{:S(2)}) async-start(), calls=%async_computation.4 | async-start | bytes 12976128 | tf_op jit(solution)/shard_map/all_gather | solution.py:119
  35.5 74.4 %all-to-all-start = ((f32[32,56,256]{2,1,0:T(8,128)}), f32[32,56,256]{2,1,0:T(8,128)S(1)}, u32[]{:S(2)}, u32[]{:S(2)}) async-start(f32[32,56,256]{2,1,0:T(8,128)} %pad_maximum_fusion.1), calls=%async_computation | async-start | bytes 3670016 | tf_op jit(solution)/shard_map/all_to_all | solution.py:130
  186.0 1.9 copy-start.3
  190.5 169.4 %all-to-all-start.2 = ((f32[32,128,256]{2,1,0:T(8,128)}), f32[32,128,256]{2,1,0:T(8,128)}, u32[]{:S(2)}, u32[]{:S(2)}) async-start(f32[32,128,256]{2,1,0:T(8,128)} %bitcast.126), calls=%async_computation.2 | async-start | bytes 8388608 | tf_op jit(solution)/shard_map/all_to_all | solution.py:139
  194.1 312.5 %all-gather.4.cloned.1.call-start = ((), (), s32[]{:S(2)}) async-start(), calls=%async_computation.3 | async-start | bytes 17301504 | tf_op jit(solution)/shard_map/all_gather | solution.py:160
  209.2 1.8 copy-start.4
  221.3 14.0 %copy-start.2 = (f32[32,128,512]{2,1,0:T(8,128)}, f32[32,128,512]{2,1,0:T(8,128)S(1)}, u32[]{:S(2)}) copy-start(f32[32,128,512]{2,1,0:T(8,128)S(1)} %slice_add_fusion) | copy-start | bytes 25165828
  235.3 36.7 %copy-start.5 = (s32[2]{0:T(128)S(1)}, s32[2]{0:T(128)}, u32[]{:S(2)}) copy-start(s32[2]{0:T(128)} %iota_multiply_fusion) | copy-start | bytes 28
  506.6 15.0 %slice-start = ((s8[16777216]{0:T(1024)(128)(4,1)}), s8[4194304]{0:T(1024)(128)(4,1)S(1)}, s32[]{:S(2)}) async-start(s8[16777216]{0:T(1024)(128)(4,1)} %bitcast.123), calls=%async_computation.5 | async-start | bytes 8388608
  506.6 15.0 %slice-start.1 = ((s8[16777216]{0:T(1024)(128)(4,1)}), s8[4194304]{0:T(1024)(128)(4,1)S(1)}, s32[]{:S(2)}) async-start(s8[16777216]{0:T(1024)(128)(4,1)} %bitcast.123), calls=%async_computation.6 | async-start | bytes 8388608
  506.6 15.0 %slice-start.2 = ((s8[16777216]{0:T(1024)(128)(4,1)}), s8[4194304]{0:T(1024)(128)(4,1)S(1)}, s32[]{:S(2)}) async-start(s8[16777216]{0:T(1024)(128)(4,1)} %bitcast.123), calls=%async_computation.7 | async-start | bytes 8388608
  519.2 3.7 slice-start.3
  522.9 6.4 %copy-start.1 = (bf16[4,48,8192]{2,1,0:T(8,128)(2,1)S(1)}, bf16[4,48,8192]{2,1,0:T(8,128)(2,1)}, u32[]{:S(2)}) copy-start(bf16[4,48,8192]{2,1,0:T(8,128)(2,1)} %param.10) | copy-start | bytes 9437188
Sparse Core Ops, SparseCore 0:
  30.0 149.2 all-gather.5
  378.6 128.0 all-gather.3

commit v2 on v1

--- a/solution.py
+++ b/solution.py
@@ -73,6 +73,26 @@
 def lower_inverse(factor):
     unit = jnp.eye(factor.shape[0], dtype=jnp.float32)
     return jax.scipy.linalg.solve_triangular(factor, unit, lower=True)
+
+
+def factored(gram):
+    size = gram.shape[0]
+    half = size // 2
+    inverse_a = lower_inverse(jnp.linalg.cholesky(gram[:half, :half]))
+    upper_a = dot(inverse_a, gram[:half])
+    side = upper_a[:, half:size]
+    left = gram[half:] - dot_t(side, upper_a)
+    inverse_b = lower_inverse(jnp.linalg.cholesky(left[:, half:size]))
+    upper_b = dot(inverse_b, left)
+    corner = -dot(inverse_b, dot_t(side, inverse_a))
+    inverse = jnp.concatenate(
+        [
+            jnp.concatenate([inverse_a, jnp.zeros((half, size - half), jnp.float32)], 1),
+            jnp.concatenate([corner, inverse_b], 1),
+        ],
+        0,
+    )
+    return inverse, jnp.concatenate([upper_a, upper_b], 0)
 
 
 def local(initial_carry, forcing, transition, partials, arc_of_row, counts):
@@ -150,9 +170,9 @@
     )
     panels = panels.reshape(epochs * rows, head)
     gram = dot_t(panels, panels)
-    inverse0 = lower_inverse(jnp.linalg.cholesky(gram[:PANEL, :PANEL]))
-    cross = dot(inverse0, gram[:PANEL, PANEL:])
-    inverse1 = lower_inverse(jnp.linalg.cholesky(gram[PANEL:, PANEL:] - dot_t(cross, cross)))
+    inverse0, upper0 = factored(gram[:PANEL])
+    cross = upper0[:, PANEL:]
+    inverse1, _ = factored(gram[PANEL:, PANEL:] - dot_t(cross, cross))
 
     products = dot_t(panels, shares)
     upper = dot(inverse0, products[:PANEL])

time: 544 us -> 516 us (0.949)
  other arithmetic: 125 us -> 108 us
  local copies, waits for them, and re-layouts: 44.9 us -> 35.1 us
    another operation x13 -> x12, other arithmetic: 69.2 us -> 50.5 us  [the longest x6 25.5 us: factored(): inverse_b = lower_inverse(jnp.linalg.cholesky(left[:, half:size]))]
    another operation x15 -> x2, local copies, waits for them, and re-layouts: 8.58 us -> 0.18 us  [lower_inverse(): return jax.scipy.linalg.solve_triangular(factor, unit, lower=True)]
    another operation x5 -> x8, other arithmetic: 40.1 us -> 42 us  [lower_inverse(): return jax.scipy.linalg.solve_triangular(factor, unit, lower=True)]
    dot_general x4 -> x8, matrix products: 31.5 us -> 33.1 us  [dot_t(): lax.dot_general(a, b, (((0,), (0,)), ((), ())), precision=HIGH, preferred...]
    dot_general x13 -> x17, matrix products: 31.9 us -> 33.1 us  [dot(): return jnp.dot(a, b, precision=HIGH, preferred_element_type=jnp.float32)]
  transfers between devices with their start and end apart: 4 -> 4, of which waited for: 2 -> 2; matrix products, arithmetic and copies ran while one was open for 34% -> 30% of each run, Pallas kernels for 1% -> 1%
where the time goes in v2:
time: 516 us; the launch traced here: 508 us
  waiting for transfers between devices  192 us (37%)
  other arithmetic  108 us (21%)
  matrix products  77.2 us (15%)
  blocking collectives  67.4 us (13%)
  local copies, waits for them, and re-layouts  35.1 us (7%)
  between operations  15.1 us (3%)
  starting transfers between devices  11.5 us (2%)
    all_gather x1, waiting for transfers between devices, local(): lax.all_gather(jnp.concatenate([upper, lower], 0), 'epoch', axis=1, tiled...  125 us
    all_to_all x1, blocking collectives, local(): incoming = lax.all_to_all(before, 'epoch', 0, 0)  67.4 us
    all_to_all x1, waiting for transfers between devices, local(): arrived = lax.all_to_all(outgoing, 'epoch', 0, 0)  66.3 us
    another operation x8, other arithmetic, lower_inverse(): return jax.scipy.linalg.solve_triangular(factor, unit, lower=True)  42 us
    dot_general x17, matrix products, dot(): return jnp.dot(a, b, precision=HIGH, preferred_element_type=jnp.float32)  33.1 us
    dot_general x8, matrix products, dot_t(): lax.dot_general(a, b, (((0,), (0,)), ((), ())), precision=HIGH, preferred...  33.1 us
    another operation x6, other arithmetic, factored(): inverse_b = lower_inverse(jnp.linalg.cholesky(left[:, half:size]))  25.5 us
    another operation x6, other arithmetic, factored(): inverse_a = lower_inverse(jnp.linalg.cholesky(gram[:half, :half]))  24.9 us
  transfers between devices with their start and end apart: 4, of which 2 were waited for; matrix products, arithmetic and copies ran while one was open for 30% of the time, Pallas kernels for 1%

profile of v2, /device:TPU:0, one launch (start us, length us, event | category | flops | bytes accessed | tf_op | source)
XLA Modules:
  0.0 508.3 jit_solution(18429038442268893998)
XLA Ops:
  7.8 1.0 fusion.92
  11.0 1.1 copy.54
  13.2 1.6 squeeze.12
  14.8 1.6 squeeze.15
  17.2 1.0 fusion.81
  18.3 1.0 fusion.85
  19.3 1.0 fusion.73
  20.3 1.0 fusion.77
  22.1 5.9 %fusion.10 = f32[176,8192]{1,0:T(8,128)} fusion(bf16[192,8192]{1,0:T(8,128)(2,1)S(1)} %bitcast.104, f32[48,48]{0,1:T(8,128)} %fusion.89, f32[32,48]{0,1:T(8,128)} %get-tuple-element.9, f32[96,48]{0,1:T(8,128)S(1)} %broadcast_in_dim.20, f32[80,48]{0,1:T(8,128)S(1)} %fusion.81, f32[32,48]{0,1:T(8,128)} %get-tuple-element.10, ...), kind=kOutput, calls=%fused_computation.31 | convolution fusion | flops 3322226688 | bytes 9048064 | tf_op jit(solution)/shard_map/dot_general | solution.py:16
  28.0 1.0 slice.211
  29.9 2.7 slice.205
  32.5 1.6 copy.102
  34.1 1.4 pad_maximum_fusion.1
  35.5 7.3 %all-to-all-start = ((f32[32,56,256]{2,1,0:T(8,128)}), f32[32,56,256]{2,1,0:T(8,128)S(1)}, u32[]{:S(2)}, u32[]{:S(2)}) async-start(f32[32,56,256]{2,1,0:T(8,128)} %pad_maximum_fusion.1), calls=%async_computation | async-start | bytes 3670016 | tf_op jit(solution)/shard_map/all_to_all | solution.py:150
  43.6 66.3 %all-to-all-done = f32[32,56,256]{2,1,0:T(8,128)S(1)} async-done(((f32[32,56,256]{2,1,0:T(8,128)}), f32[32,56,256]{2,1,0:T(8,128)S(1)}, u32[]{:S(2)}, u32[]{:S(2)}) %all-to-all-start) | async-done | bytes 1835040 | tf_op jit(solution)/shard_map/all_to_all | solution.py:150
  110.8 1.4 broadcast_in_dim.46.map_ref
  112.2 0.9 shard_map.77
  113.1 67.4 %all_to_all.15 = f32[32,48,256]{2,1,0:T(8,128)S(1)} all-to-all(f32[32,48,256]{2,1,0:T(8,128)S(1)} %shard_map.77), channel_id=1, replica_groups=mesh['epoch'=32,'param'=1] {'epoch'}, dimensions={0} | all-to-all | bytes 3145728 | tf_op jit(solution)/shard_map/all_to_all | solution.py:155
  180.7 5.3 %convolution_add_fusion = f32[128,8192]{1,0:T(8,128)S(1)} fusion(f32[48,8192]{1,0:T(8,128)S(1)} %bitcast.114, f32[176,8192]{1,0:T(8,128)} %fusion.10, f32[176,48]{0,1:T(8,128)S(1)} %fusion.77), kind=kOutput, calls=%fused_computation.2 | convolution fusion | flops 605028352 | bytes 9986048 | tf_op jit(solution)/shard_map/dot_general | solution.py:16
  186.0 1.9 copy-done.3
  187.9 2.6 copy.101
  190.5 3.6 all-to-all-start.2
  194.7 0.9 slice.175.start_ref
  195.6 1.3 slice.213
  197.5 0.9 slice.214
  198.5 2.3 slice.216.shift_ref
  200.9 1.1 copy.63
  202.0 3.1 reshape.130
  205.0 2.3 broadcast_in_dim.48.map_ref
  207.4 1.8 shard_map.78
  209.2 9.9 %slice_add_fusion = f32[32,128,512]{2,1,0:T(8,128)S(1)} fusion(f32[32,192,512]{2,1,0:T(8,128)} %bitcast.111, f32[32,128,48]{2,1,0:T(8,128)S(1)} %copy-done.4, f32[32,48,512]{2,1,0:T(8,128)S(1)} %shard_map.78), kind=kOutput, calls=%fused_computation.4 | convolution fusion | flops 1210056704 | bytes 20709376 | tf_op jit(solution)/shard_map/prk,pkc->prc/dot_general | solution.py:168
  219.2 14.0 %convolution_bitcast_fusion = f32[512,512]{1,0:T(8,128)S(1)} fusion(f32[32,128,512]{2,1,0:T(8,128)S(1)} %slice_add_fusion), kind=kOutput, calls=%fused_computation.10 | convolution fusion | flops 12884901888 | bytes 9437184 | tf_op jit(solution)/shard_map/dot_general | solution.py:20
  233.4 11.7 %cholesky.74 = f32[128,128]{1,0:T(8,128)S(1)} custom-call(f32[128,128]{1,0:T(8,128)S(1)} %fusion.65), custom_call_target="Cholesky" | custom-call | tf_op jit(solution)/shard_map/jit(cholesky)/cholesky | solution.py:81
  246.6 9.8 %custom-call.8 = f32[1,128,128]{1,2,0:T(8,128)S(1)} custom-call(f32[1,128,128]{2,1,0:T(8,128)S(1)} %fusion.54), custom_call_target="InvertDiagBlocksLowerTriangular" | custom-call | tf_op jit(solution)/shard_map/jit(_solve_triangular)/triangular_solve | solution.py:75
  258.1 12.2 %cholesky.85 = f32[128,128]{1,0:T(8,128)S(1)} custom-call(f32[128,128]{1,0:T(8,128)S(1)} %fusion.63), custom_call_target="Cholesky" | custom-call | tf_op jit(solution)/shard_map/jit(cholesky)/cholesky | solution.py:85
  271.7 9.8 %custom-call.9 = f32[1,128,128]{1,2,0:T(8,128)S(1)} custom-call(f32[1,128,128]{2,1,0:T(8,128)S(1)} %fusion.55), custom_call_target="InvertDiagBlocksLowerTriangular" | custom-call | tf_op jit(solution)/shard_map/jit(_solve_triangular)/triangular_solve | solution.py:75
  283.1 11.7 %cholesky.96 = f32[128,128]{1,0:T(8,128)S(1)} custom-call(f32[128,128]{1,0:T(8,128)S(1)} %fusion.61), custom_call_target="Cholesky" | custom-call | tf_op jit(solution)/shard_map/jit(cholesky)/cholesky | solution.py:81
  296.3 9.8 %custom-call.10 = f32[1,128,128]{1,2,0:T(8,128)S(1)} custom-call(f32[1,128,128]{2,1,0:T(8,128)S(1)} %fusion.56), custom_call_target="InvertDiagBlocksLowerTriangular" | custom-call | tf_op jit(solution)/shard_map/jit(_solve_triangular)/triangular_solve | solution.py:75
  307.2 11.9 %cholesky.107 = f32[128,128]{1,0:T(8,128)S(1)} custom-call(f32[128,128]{1,0:T(8,128)S(1)} %fusion.59), custom_call_target="Cholesky" | custom-call | tf_op jit(solution)/shard_map/jit(cholesky)/cholesky | solution.py:85
  320.5 9.8 %custom-call.11 = f32[1,128,128]{1,2,0:T(8,128)S(1)} custom-call(f32[1,128,128]{2,1,0:T(8,128)S(1)} %fusion.57), custom_call_target="InvertDiagBlocksLowerTriangular" | custom-call | tf_op jit(solution)/shard_map/jit(_solve_triangular)/triangular_solve | solution.py:75
  331.9 16.3 %convolution_bitcast_fusion.1 = f32[512,256]{1,0:T(8,128)S(1)} fusion(f32[32,128,512]{2,1,0:T(8,128)} %copy-done.2, f32[32,128,256]{2,1,0:T(8,128)} %all-to-all-done.2), kind=kOutput, calls=%fused_computation.11 | convolution fusion | flops 6442450944 | bytes 13107200 | tf_op jit(solution)/shard_map/dot_general | solution.py:20
  350.4 1.3 fusion.32
  351.7 1.2 convolution_subtract_fusion.3
  353.3 125.3 %all-gather.4.cloned.1.call-done = f32[512,8192]{1,0:T(8,128)} async-done(((f32[512,256]{1,0:T(8,128)}), f32[512,8192]{1,0:T(8,128)}) %all-gather.4.cloned.1.call-update) | async-done | bytes 16777232 | tf_op jit(solution)/shard_map/all_gather | solution.py:180
  478.6 12.6 %fusion.2 = f32[128,7680]{1,0:T(8,128)S(1)} fusion(f32[512,8192]{1,0:T(8,128)} %all-gather.4.cloned.1.call-done, f32[128,8192]{1,0:T(8,128)} %copy-done.3, f32[128,256]{1,0:T(8,128)S(1)} %fusion.34, f32[128,256]{1,0:T(8,128)S(1)} %fusion.32), kind=kOutput, calls=%fused_computation.3 | convolution fusion | flops 6040846336 | bytes 23855104 | tf_op jit(solution)/shard_map/dot_general | solution.py:16
  491.2 2.4 pad_maximum_fusion
  493.6 1.3 slice-done.3
  494.9 6.4 %broadcast_multiply_fusion = f32[512,8192]{1,0:T(8,128)} fusion(f32[512,8192]{1,0:T(8,128)S(1)} %bitcast.106), kind=kLoop, calls=%fused_computation.5 | loop fusion | flops 4194304 | bytes 33554432 | tf_op jit(solution)/shard_map/div | solution.py:195
  (112 shorter events, 23.6 us)
Async XLA Ops:
  7.2 14.9 %copy-start = (bf16[4,48,8192]{2,1,0:T(8,128)(2,1)S(1)}, bf16[4,48,8192]{2,1,0:T(8,128)(2,1)}, u32[]{:S(2)}) copy-start(bf16[4,48,8192]{2,1,0:T(8,128)(2,1)} %param.10) | copy-start | bytes 9437188
  7.2 188.4 %all-gather.6.cloned.1.call-start = ((), (), s32[]{:S(2)}) async-start(), calls=%async_computation.4 | async-start | bytes 12976128 | tf_op jit(solution)/shard_map/all_gather | solution.py:139
  35.5 74.4 %all-to-all-start = ((f32[32,56,256]{2,1,0:T(8,128)}), f32[32,56,256]{2,1,0:T(8,128)S(1)}, u32[]{:S(2)}, u32[]{:S(2)}) async-start(f32[32,56,256]{2,1,0:T(8,128)} %pad_maximum_fusion.1), calls=%async_computation | async-start | bytes 3670016 | tf_op jit(solution)/shard_map/all_to_all | solution.py:150
  186.0 1.9 copy-start.3
  190.5 141.4 %all-to-all-start.2 = ((f32[32,128,256]{2,1,0:T(8,128)}), f32[32,128,256]{2,1,0:T(8,128)}, u32[]{:S(2)}, u32[]{:S(2)}) async-start(f32[32,128,256]{2,1,0:T(8,128)} %bitcast.108), calls=%async_computation.2 | async-start | bytes 8388608 | tf_op jit(solution)/shard_map/all_to_all | solution.py:159
  194.1 284.5 %all-gather.4.cloned.1.call-start = ((), (), s32[]{:S(2)}) async-start(), calls=%async_computation.3 | async-start | bytes 17301504 | tf_op jit(solution)/shard_map/all_gather | solution.py:180
  207.4 1.8 copy-start.4
  219.2 14.1 %copy-start.2 = (f32[32,128,512]{2,1,0:T(8,128)}, f32[32,128,512]{2,1,0:T(8,128)S(1)}, u32[]{:S(2)}) copy-start(f32[32,128,512]{2,1,0:T(8,128)S(1)} %slice_add_fusion) | copy-start | bytes 25165828
  478.6 15.0 %slice-start = ((s8[16777216]{0:T(1024)(128)(4,1)}), s8[4194304]{0:T(1024)(128)(4,1)S(1)}, s32[]{:S(2)}) async-start(s8[16777216]{0:T(1024)(128)(4,1)} %bitcast.105), calls=%async_computation.5 | async-start | bytes 8388608
  478.6 15.0 %slice-start.1 = ((s8[16777216]{0:T(1024)(128)(4,1)}), s8[4194304]{0:T(1024)(128)(4,1)S(1)}, s32[]{:S(2)}) async-start(s8[16777216]{0:T(1024)(128)(4,1)} %bitcast.105), calls=%async_computation.6 | async-start | bytes 8388608
  478.6 15.0 %slice-start.2 = ((s8[16777216]{0:T(1024)(128)(4,1)}), s8[4194304]{0:T(1024)(128)(4,1)S(1)}, s32[]{:S(2)}) async-start(s8[16777216]{0:T(1024)(128)(4,1)} %bitcast.105), calls=%async_computation.7 | async-start | bytes 8388608
  491.2 3.7 slice-start.3
  494.9 6.4 %copy-start.1 = (bf16[4,48,8192]{2,1,0:T(8,128)(2,1)S(1)}, bf16[4,48,8192]{2,1,0:T(8,128)(2,1)}, u32[]{:S(2)}) copy-start(bf16[4,48,8192]{2,1,0:T(8,128)(2,1)} %param.10) | copy-start | bytes 9437188
Sparse Core Ops, SparseCore 0:
  30.0 149.2 all-gather.5
  350.5 128.0 all-gather.3
